TPU v7x, 32 devices: a whole 2x2x4 slice. The times are simulated.
32 devices in a mesh: replica: 2 (over y), pool: 4 (over z), tensor: 2 (over x), seq: 2 (over core).
Axes of the slice: x: 2, y: 2, z: 4, core: 2. Of those that a mesh axis runs over, the one named last changes fastest.
Arguments:
- queries: bfloat16 [8, 256, 32, 128], P(('replica', 'pool'), 'seq', 'tensor'), parts along dimension 0
- suffix_kv: bfloat16 [8, 2, 256, 8, 128], P(('replica', 'pool'), None, 'seq', 'tensor'), parts along dimension 0
- page_store: bfloat16 [256, 2, 8, 128, 128], P(('replica', 'pool'), None, ('tensor', 'seq')), parts along dimension 0
- holder_table: int32 [8, 8, 2], P('replica'), parts along dimension 0, may hold values from 0 to 31, as said below
- prefix_pages: int32 [8], P('replica'), parts along dimension 0, may hold values from 1 to 8, 20 in all
- suffix_pages: int32 [8], P('replica'), parts along dimension 0, may hold values from 1 to 2, 6 in all
- fresh_alloc: int32 [8, 2, 2], P('replica'), parts along dimension 0, may hold values from 0 to 3, as said below
Outputs:
- attention: bfloat16 [8, 256, 32, 128], P(('replica', 'pool'), 'seq', 'tensor'), parts along dimension 0
- row_lse: float32 [8, 32, 256], P(('replica', 'pool'), 'tensor', 'seq'), parts along dimension 0
- fresh_store: bfloat16 [16, 2, 8, 128, 128], P(('replica', 'pool'), None, ('tensor', 'seq')), parts along dimension 0
There are 2 independent parts, one for each index of `replica`. A program takes and returns all parts, laid end to end along the dimension named above; each array names one. Nothing has to cross between parts.
Inputs may be any that keep to these rules, and one draw needn't show every extreme that they name: `holder_table`: entry [r, p, 0] is a holder below 4 and entry [r, p, 1] a slot below 32. Over the 8 entries of one request each holder is named exactly 2 times, so a request with 8 prefix pages takes 2 pages from every holder. `fresh_alloc`: entry [r, q] holds a holder below 4 and the slot q; every pair of holder and slot below 2 is named by exactly one entry, and the 2 pages of one request go to 2 different holders. `prefix_pages`: some request has 8 prefix pages. `suffix_pages`: some request has 2 suffix pages.
All inputs are finite; a program needn't handle non-finite values.
Results may differ from a plain program's by a relative error of at most 0.0051.
Values may be sent and summed in bfloat16 or wider, within the bound.
A program may use at most 64 MiB of HBM per device.

v0:
```python
import jax
import jax.numpy as jnp
from jax import lax
from jax.sharding import PartitionSpec as P


def passed_along(block, axis, distance):
    devices = range(lax.axis_size(axis))
    route = [(i - distance, i) for i in devices if i - distance in devices]
    return lax.ppermute(block, axis, route)


def attend(query_rows, key_all, visible, group_size):
    head_dim = query_rows.shape[2]

    def one_head(head):
        query_head = lax.dynamic_index_in_dim(query_rows, head, 1, keepdims=False)
        kv_index = head // group_size
        keys_head = lax.dynamic_index_in_dim(key_all[0], kv_index, 0, keepdims=False)
        values_head = lax.dynamic_index_in_dim(key_all[1], kv_index, 0, keepdims=False)
        scores = jnp.einsum(
            "rd,kd->rk", query_head, keys_head, preferred_element_type=jnp.float32
        ) * head_dim ** (-0.5)
        scores = jnp.where(visible, scores, -jnp.inf)
        row_max = jnp.max(scores, axis=1, keepdims=True)
        log_total = row_max[:, 0] + jnp.log(jnp.sum(jnp.exp(scores - row_max), axis=1))
        weights = jnp.exp(scores - log_total[:, None]).astype(jnp.bfloat16)
        result = jnp.dot(weights, values_head, preferred_element_type=jnp.float32)
        return (result, log_total)

    return lax.map(one_head, jnp.arange(query_rows.shape[1]))


def body(queries, suffix_kv, page_store, holder_table, prefix_pages, suffix_pages, fresh_alloc):
    pool_count = lax.axis_size("pool")
    seq_count = lax.axis_size("seq")
    holder_index = lax.axis_index("pool")
    seq_index = lax.axis_index("seq")
    slots_dev, _, kv_dev, page_len, head_dim = page_store.shape
    requests, prefix_cap = (holder_table.shape[0], holder_table.shape[1])
    capacity = prefix_cap // pool_count
    row_count = queries.shape[1]
    query_dev = queries.shape[2]
    group_size = query_dev // (kv_dev * seq_count)
    holders = holder_table[:, :, 0]
    slot_ids = holder_table[:, :, 1]
    position = jnp.arange(prefix_cap, dtype=jnp.int32)
    live_pages = position[None, :] < prefix_pages[:, None]
    same_holder = holders[:, :, None] == holders[:, None, :]
    before = position[None, :] < position[:, None]
    ranks = jnp.sum((same_holder & before[None]).astype(jnp.int32), axis=2)
    own_pages = live_pages & (holders == holder_index)
    levels = jnp.arange(capacity, dtype=jnp.int32)
    picked = own_pages[:, None, :] & (ranks[:, None, :] == levels[None, :, None])
    slot_index = jnp.sum(jnp.where(picked, slot_ids[:, None, :], 0), axis=2)
    outgoing = jnp.take(page_store, slot_index.reshape(-1), axis=0)
    outgoing = outgoing.reshape(requests, capacity, 2, kv_dev, page_len, head_dim)
    outgoing = jnp.transpose(outgoing, (2, 3, 0, 1, 4, 5))
    holders_mine = lax.dynamic_index_in_dim(holders, holder_index, 0, keepdims=False)
    prefix_mine = lax.dynamic_index_in_dim(prefix_pages, holder_index, 0, keepdims=False)
    live_mine = position < prefix_mine
    pool_ids = jnp.arange(pool_count, dtype=jnp.int32)
    counts = jnp.sum(
        (live_mine[None, :] & (holders_mine[None, :] == pool_ids[:, None])).astype(jnp.int32),
        axis=1,
    )
    filled = levels[None, :] < counts[:, None]
    prefix_ok = jnp.broadcast_to(filled[:, :, None], (pool_count, capacity, page_len)).reshape(-1)
    suffix_heads = lax.all_to_all(suffix_kv, "seq", split_axis=3, concat_axis=2, tiled=True)
    total_rows = suffix_heads.shape[2]
    spages = total_rows // page_len
    fresh_pages = suffix_heads[0].reshape(2, spages, page_len, kv_dev, head_dim)
    fresh_pages = jnp.transpose(fresh_pages, (0, 3, 1, 2, 4))
    suffix_mine = lax.dynamic_index_in_dim(suffix_pages, holder_index, 0, keepdims=False)
    alloc_mine = lax.dynamic_index_in_dim(fresh_alloc, holder_index, 0, keepdims=False)
    spage_ids = jnp.arange(spages, dtype=jnp.int32)
    send_select = (alloc_mine[:, 0][None, :] == pool_ids[:, None]) & (spage_ids < suffix_mine)[
        None, :
    ]
    push_out = jnp.einsum(
        "dq,akqph->akdph",
        send_select.astype(jnp.bfloat16),
        fresh_pages,
        preferred_element_type=jnp.float32,
    ).astype(jnp.bfloat16)
    push_out = push_out[:, :, :, None]
    arrived = lax.all_to_all(outgoing, "pool", split_axis=2, concat_axis=2, tiled=True)
    landed = lax.all_to_all(push_out, "pool", split_axis=2, concat_axis=2, tiled=True)
    source_live = spage_ids[None, :] < suffix_pages[:, None]
    fresh_ids = jnp.arange(spages, dtype=jnp.int32)
    select = (fresh_alloc[:, :, 0] == holder_index)[None] & source_live[None]
    select = select & (fresh_alloc[:, :, 1][None] == fresh_ids[:, None, None])
    receive_select = jnp.any(select, axis=2)
    fresh_store = jnp.einsum(
        "fr,akrph->fakph",
        receive_select.astype(jnp.bfloat16),
        landed[:, :, :, 0],
        preferred_element_type=jnp.float32,
    ).astype(jnp.bfloat16)
    prefix_rows = pool_count * capacity * page_len
    pages_all = lax.all_gather(arrived, "seq", axis=1, tiled=True)
    kv_tensor = pages_all.shape[1]
    lower_rows = passed_along(suffix_kv, "seq", 1)
    prefix_kv = pages_all.reshape(2, kv_tensor, prefix_rows, head_dim)
    suffix_keys = jnp.transpose(
        jnp.concatenate([lower_rows[0], suffix_kv[0]], axis=1), (0, 2, 1, 3)
    )
    key_all = jnp.concatenate([prefix_kv, suffix_keys], axis=2)
    local_ids = jnp.arange(row_count, dtype=jnp.int32)
    lower_seen = jnp.broadcast_to(seq_index > 0, (row_count, row_count))
    causal = local_ids[None, :] <= local_ids[:, None]
    visible = jnp.concatenate(
        [jnp.broadcast_to(prefix_ok[None, :], (row_count, prefix_rows)), lower_seen, causal], axis=1
    )
    result, log_total = attend(queries[0], key_all, visible, group_size)
    live_rows = seq_index * row_count + local_ids < suffix_mine * page_len
    result = jnp.where(live_rows[None, :, None], result, 0.0).astype(jnp.bfloat16)
    log_total = jnp.where(live_rows[None, :], log_total, 0.0)
    attention = jnp.transpose(result, (1, 0, 2))[None]
    row_lse = log_total[None]
    return (attention, row_lse, fresh_store)


def solution(mesh):
    placed = (
        P(("replica", "pool"), "seq", "tensor", None),
        P(("replica", "pool"), None, "seq", "tensor", None),
        P(("replica", "pool"), None, ("tensor", "seq"), None, None),
        P("replica", None, None),
        P("replica"),
        P("replica"),
        P("replica", None, None),
    )
    return jax.shard_map(
        body,
        mesh=mesh,
        in_specs=placed,
        out_specs=(
            P(("replica", "pool"), "seq", "tensor", None),
            P(("replica", "pool"), "tensor", "seq"),
            P(("replica", "pool"), None, ("tensor", "seq"), None, None),
        ),
        check_vma=False,
    )
```

profile of v0, /device:TPU:0, one launch (start us, length us, event | category | flops | bytes accessed | tf_op | source)
XLA Modules:
  0.0 236.0 jit_solution(4745524647614569631)
XLA Ops:
  7.2 1.7 copy.86
  8.9 3.4 %all-to-all-start.1 = ((bf16[1,2,128,4,128]{4,2,1,0,3:T(8,128)(2,1)}), bf16[1,2,128,4,128]{4,2,1,0,3:T(8,128)(2,1)S(1)}, u32[]{:S(2)}, u32[]{:S(2)}) async-start(bf16[1,2,128,4,128]{4,2,1,0,3:T(8,128)(2,1)} %copy.86), calls=%async_computation.1 | async-start | bytes 524288 | tf_op jit(solution)/shard_map/all_to_all | solution.py:69
  14.5 2.9 %gather_fusion = bf16[8,2,2,128,128]{4,3,2,1,0:T(8,128)(2,1)S(1)} fusion(bf16[32,2,2,128,128]{4,3,2,1,0:T(8,128)(2,1)} %param.11, s32[1024]{0:T(1024)S(1)} %pad_clamp_fusion), kind=kCustom, calls=%fused_computation | custom fusion | bytes 2097184 | tf_op jit(solution)/shard_map/jit(_take)/gather | solution.py:56
  18.7 6.3 %all-to-all-start = ((bf16[2,2,4,2,128,128]{5,4,3,1,0,2:T(8,128)(2,1)}), bf16[2,2,4,2,128,128]{5,4,3,1,0,2:T(8,128)(2,1)S(1)}, u32[]{:S(2)}, u32[]{:S(2)}) async-start(bf16[2,2,4,2,128,128]{5,4,3,1,0,2:T(8,128)(2,1)} %copy.77), calls=%async_computation | async-start | bytes 2097152 | tf_op jit(solution)/shard_map/all_to_all | solution.py:87
  25.1 2.1 collective-permute-start
  31.6 19.8 %all-to-all-done = bf16[2,2,4,2,128,128]{5,4,3,1,0,2:T(8,128)(2,1)S(1)} async-done(((bf16[2,2,4,2,128,128]{5,4,3,1,0,2:T(8,128)(2,1)}), bf16[2,2,4,2,128,128]{5,4,3,1,0,2:T(8,128)(2,1)S(1)}, u32[]{:S(2)}, u32[]{:S(2)}) %all-to-all-start) | async-done | bytes 1048608 | tf_op jit(solution)/shard_map/all_to_all | solution.py:87
  51.4 3.5 %all-to-all-start.2 = ((bf16[2,2,4,1,128,128]{5,4,1,0,3,2:T(8,128)(2,1)}), bf16[2,2,4,1,128,128]{5,4,1,0,3,2:T(8,128)(2,1)S(1)}, u32[]{:S(2)}, u32[]{:S(2)}) async-start(bf16[2,2,4,1,128,128]{5,4,1,0,3,2:T(8,128)(2,1)} %copy.89), calls=%async_computation.2 | async-start | bytes 1048576 | tf_op jit(solution)/shard_map/all_to_all | solution.py:88
  58.3 10.9 %all-to-all-done.2 = bf16[2,2,4,1,128,128]{5,4,1,0,3,2:T(8,128)(2,1)S(1)} async-done(((bf16[2,2,4,1,128,128]{5,4,1,0,3,2:T(8,128)(2,1)}), bf16[2,2,4,1,128,128]{5,4,1,0,3,2:T(8,128)(2,1)S(1)}, u32[]{:S(2)}, u32[]{:S(2)}) %all-to-all-start.2) | async-done | bytes 524320 | tf_op jit(solution)/shard_map/all_to_all | solution.py:88
  70.4 1.8 pad_maximum_fusion
  72.2 154.3 %while.15 = (s32[]{:T(128)}, bf16[16,128,128]{2,0,1:T(8,128)(2,1)}, f32[16,128]{1,0:T(8,128)S(1)}, s32[16]{0:T(128)S(1)}, bf16[128,16,128]{2,0,1:T(8,128)(2,1)},...) while((s32[]{:T(128)}, bf16[16,128,128]{2,0,1:T(8,128)(2,1)}, ...), condition=%wide.region_6.7_spmd.clone, body=%wide.region_3.6_spmd.sunk.clone | while | flops 85032848 | bytes 8262462 | solution.py:31
  78.9 2.9 %dynamic_update_slice.18 = bf16[16,128,128]{2,0,1:T(8,128)(2,1)} dynamic-update-slice(bf16[16,128,128]{2,0,1:T(8,128)(2,1)} %get-tuple-element.265, f32[1,128,128]{2,0,1:T(1,128)S(1)} %bitcast.91, s32[]{:T(128)} %get-tuple-element.264, s32[]{:T(128)} %constant.122.clone.1..sunk.1, s32[]{:T(128)} %constant.122.clone.1..sunk.1) | dynamic-update-slice | bytes 131076 | tf_op jit(solution)/shard_map/while/body/jit(dynamic_update_index_in_dim)/dynamic_update_slice | solution.py:31
  86.9 1.1 fusion.46
  88.6 2.9 %dynamic_update_slice.18 = bf16[16,128,128]{2,0,1:T(8,128)(2,1)} dynamic-update-slice(bf16[16,128,128]{2,0,1:T(8,128)(2,1)} %get-tuple-element.265, f32[1,128,128]{2,0,1:T(1,128)S(1)} %bitcast.91, s32[]{:T(128)} %get-tuple-element.264, s32[]{:T(128)} %constant.122.clone.1..sunk.1, s32[]{:T(128)} %constant.122.clone.1..sunk.1) | dynamic-update-slice | bytes 131076 | tf_op jit(solution)/shard_map/while/body/jit(dynamic_update_index_in_dim)/dynamic_update_slice | solution.py:31
  96.5 1.1 fusion.46
  98.2 2.9 %dynamic_update_slice.18 = bf16[16,128,128]{2,0,1:T(8,128)(2,1)} dynamic-update-slice(bf16[16,128,128]{2,0,1:T(8,128)(2,1)} %get-tuple-element.265, f32[1,128,128]{2,0,1:T(1,128)S(1)} %bitcast.91, s32[]{:T(128)} %get-tuple-element.264, s32[]{:T(128)} %constant.122.clone.1..sunk.1, s32[]{:T(128)} %constant.122.clone.1..sunk.1) | dynamic-update-slice | bytes 131076 | tf_op jit(solution)/shard_map/while/body/jit(dynamic_update_index_in_dim)/dynamic_update_slice | solution.py:31
  107.9 2.9 %dynamic_update_slice.18 = bf16[16,128,128]{2,0,1:T(8,128)(2,1)} dynamic-update-slice(bf16[16,128,128]{2,0,1:T(8,128)(2,1)} %get-tuple-element.265, f32[1,128,128]{2,0,1:T(1,128)S(1)} %bitcast.91, s32[]{:T(128)} %get-tuple-element.264, s32[]{:T(128)} %constant.122.clone.1..sunk.1, s32[]{:T(128)} %constant.122.clone.1..sunk.1) | dynamic-update-slice | bytes 131076 | tf_op jit(solution)/shard_map/while/body/jit(dynamic_update_index_in_dim)/dynamic_update_slice | solution.py:31
  117.5 2.9 %dynamic_update_slice.18 = bf16[16,128,128]{2,0,1:T(8,128)(2,1)} dynamic-update-slice(bf16[16,128,128]{2,0,1:T(8,128)(2,1)} %get-tuple-element.265, f32[1,128,128]{2,0,1:T(1,128)S(1)} %bitcast.91, s32[]{:T(128)} %get-tuple-element.264, s32[]{:T(128)} %constant.122.clone.1..sunk.1, s32[]{:T(128)} %constant.122.clone.1..sunk.1) | dynamic-update-slice | bytes 131076 | tf_op jit(solution)/shard_map/while/body/jit(dynamic_update_index_in_dim)/dynamic_update_slice | solution.py:31
  125.4 1.1 fusion.46
  127.2 2.9 %dynamic_update_slice.18 = bf16[16,128,128]{2,0,1:T(8,128)(2,1)} dynamic-update-slice(bf16[16,128,128]{2,0,1:T(8,128)(2,1)} %get-tuple-element.265, f32[1,128,128]{2,0,1:T(1,128)S(1)} %bitcast.91, s32[]{:T(128)} %get-tuple-element.264, s32[]{:T(128)} %constant.122.clone.1..sunk.1, s32[]{:T(128)} %constant.122.clone.1..sunk.1) | dynamic-update-slice | bytes 131076 | tf_op jit(solution)/shard_map/while/body/jit(dynamic_update_index_in_dim)/dynamic_update_slice | solution.py:31
  136.8 2.9 %dynamic_update_slice.18 = bf16[16,128,128]{2,0,1:T(8,128)(2,1)} dynamic-update-slice(bf16[16,128,128]{2,0,1:T(8,128)(2,1)} %get-tuple-element.265, f32[1,128,128]{2,0,1:T(1,128)S(1)} %bitcast.91, s32[]{:T(128)} %get-tuple-element.264, s32[]{:T(128)} %constant.122.clone.1..sunk.1, s32[]{:T(128)} %constant.122.clone.1..sunk.1) | dynamic-update-slice | bytes 131076 | tf_op jit(solution)/shard_map/while/body/jit(dynamic_update_index_in_dim)/dynamic_update_slice | solution.py:31
  146.4 2.9 %dynamic_update_slice.18 = bf16[16,128,128]{2,0,1:T(8,128)(2,1)} dynamic-update-slice(bf16[16,128,128]{2,0,1:T(8,128)(2,1)} %get-tuple-element.265, f32[1,128,128]{2,0,1:T(1,128)S(1)} %bitcast.91, s32[]{:T(128)} %get-tuple-element.264, s32[]{:T(128)} %constant.122.clone.1..sunk.1, s32[]{:T(128)} %constant.122.clone.1..sunk.1) | dynamic-update-slice | bytes 131076 | tf_op jit(solution)/shard_map/while/body/jit(dynamic_update_index_in_dim)/dynamic_update_slice | solution.py:31
  156.1 2.9 %dynamic_update_slice.18 = bf16[16,128,128]{2,0,1:T(8,128)(2,1)} dynamic-update-slice(bf16[16,128,128]{2,0,1:T(8,128)(2,1)} %get-tuple-element.265, f32[1,128,128]{2,0,1:T(1,128)S(1)} %bitcast.91, s32[]{:T(128)} %get-tuple-element.264, s32[]{:T(128)} %constant.122.clone.1..sunk.1, s32[]{:T(128)} %constant.122.clone.1..sunk.1) | dynamic-update-slice | bytes 131076 | tf_op jit(solution)/shard_map/while/body/jit(dynamic_update_index_in_dim)/dynamic_update_slice | solution.py:31
  164.0 1.1 fusion.46
  165.7 2.9 %dynamic_update_slice.18 = bf16[16,128,128]{2,0,1:T(8,128)(2,1)} dynamic-update-slice(bf16[16,128,128]{2,0,1:T(8,128)(2,1)} %get-tuple-element.265, f32[1,128,128]{2,0,1:T(1,128)S(1)} %bitcast.91, s32[]{:T(128)} %get-tuple-element.264, s32[]{:T(128)} %constant.122.clone.1..sunk.1, s32[]{:T(128)} %constant.122.clone.1..sunk.1) | dynamic-update-slice | bytes 131076 | tf_op jit(solution)/shard_map/while/body/jit(dynamic_update_index_in_dim)/dynamic_update_slice | solution.py:31
  175.4 2.9 %dynamic_update_slice.18 = bf16[16,128,128]{2,0,1:T(8,128)(2,1)} dynamic-update-slice(bf16[16,128,128]{2,0,1:T(8,128)(2,1)} %get-tuple-element.265, f32[1,128,128]{2,0,1:T(1,128)S(1)} %bitcast.91, s32[]{:T(128)} %get-tuple-element.264, s32[]{:T(128)} %constant.122.clone.1..sunk.1, s32[]{:T(128)} %constant.122.clone.1..sunk.1) | dynamic-update-slice | bytes 131076 | tf_op jit(solution)/shard_map/while/body/jit(dynamic_update_index_in_dim)/dynamic_update_slice | solution.py:31
  185.0 2.9 %dynamic_update_slice.18 = bf16[16,128,128]{2,0,1:T(8,128)(2,1)} dynamic-update-slice(bf16[16,128,128]{2,0,1:T(8,128)(2,1)} %get-tuple-element.265, f32[1,128,128]{2,0,1:T(1,128)S(1)} %bitcast.91, s32[]{:T(128)} %get-tuple-element.264, s32[]{:T(128)} %constant.122.clone.1..sunk.1, s32[]{:T(128)} %constant.122.clone.1..sunk.1) | dynamic-update-slice | bytes 131076 | tf_op jit(solution)/shard_map/while/body/jit(dynamic_update_index_in_dim)/dynamic_update_slice | solution.py:31
  194.6 2.9 %dynamic_update_slice.18 = bf16[16,128,128]{2,0,1:T(8,128)(2,1)} dynamic-update-slice(bf16[16,128,128]{2,0,1:T(8,128)(2,1)} %get-tuple-element.265, f32[1,128,128]{2,0,1:T(1,128)S(1)} %bitcast.91, s32[]{:T(128)} %get-tuple-element.264, s32[]{:T(128)} %constant.122.clone.1..sunk.1, s32[]{:T(128)} %constant.122.clone.1..sunk.1) | dynamic-update-slice | bytes 131076 | tf_op jit(solution)/shard_map/while/body/jit(dynamic_update_index_in_dim)/dynamic_update_slice | solution.py:31
  202.6 1.1 fusion.46
  204.3 2.9 %dynamic_update_slice.18 = bf16[16,128,128]{2,0,1:T(8,128)(2,1)} dynamic-update-slice(bf16[16,128,128]{2,0,1:T(8,128)(2,1)} %get-tuple-element.265, f32[1,128,128]{2,0,1:T(1,128)S(1)} %bitcast.91, s32[]{:T(128)} %get-tuple-element.264, s32[]{:T(128)} %constant.122.clone.1..sunk.1, s32[]{:T(128)} %constant.122.clone.1..sunk.1) | dynamic-update-slice | bytes 131076 | tf_op jit(solution)/shard_map/while/body/jit(dynamic_update_index_in_dim)/dynamic_update_slice | solution.py:31
  213.9 2.9 %dynamic_update_slice.18 = bf16[16,128,128]{2,0,1:T(8,128)(2,1)} dynamic-update-slice(bf16[16,128,128]{2,0,1:T(8,128)(2,1)} %get-tuple-element.265, f32[1,128,128]{2,0,1:T(1,128)S(1)} %bitcast.91, s32[]{:T(128)} %get-tuple-element.264, s32[]{:T(128)} %constant.122.clone.1..sunk.1, s32[]{:T(128)} %constant.122.clone.1..sunk.1) | dynamic-update-slice | bytes 131076 | tf_op jit(solution)/shard_map/while/body/jit(dynamic_update_index_in_dim)/dynamic_update_slice | solution.py:31
  223.6 2.9 %dynamic_update_slice.18 = bf16[16,128,128]{2,0,1:T(8,128)(2,1)} dynamic-update-slice(bf16[16,128,128]{2,0,1:T(8,128)(2,1)} %get-tuple-element.265, f32[1,128,128]{2,0,1:T(1,128)S(1)} %bitcast.91, s32[]{:T(128)} %get-tuple-element.264, s32[]{:T(128)} %constant.122.clone.1..sunk.1, s32[]{:T(128)} %constant.122.clone.1..sunk.1) | dynamic-update-slice | bytes 131076 | tf_op jit(solution)/shard_map/while/body/jit(dynamic_update_index_in_dim)/dynamic_update_slice | solution.py:31
  226.5 2.0 fusion.12
  (169 shorter events, 47.9 us)
Async XLA Ops:
  8.9 9.9 %all-to-all-start.1 = ((bf16[1,2,128,4,128]{4,2,1,0,3:T(8,128)(2,1)}), bf16[1,2,128,4,128]{4,2,1,0,3:T(8,128)(2,1)S(1)}, u32[]{:S(2)}, u32[]{:S(2)}) async-start(bf16[1,2,128,4,128]{4,2,1,0,3:T(8,128)(2,1)} %copy.86), calls=%async_computation.1 | async-start | bytes 524288 | tf_op jit(solution)/shard_map/all_to_all | solution.py:69
  17.6 7.4 %copy-start = (bf16[1,2,128,4,128]{4,3,2,1,0:T(4,128)(2,1)S(1)}, bf16[1,2,128,4,128]{4,3,2,1,0:T(4,128)(2,1)}, u32[]{:S(2)}) copy-start(bf16[1,2,128,4,128]{4,3,2,1,0:T(4,128)(2,1)} %param.10) | copy-start | bytes 786436
  17.6 9.6 %copy-start.3 = (s32[4]{0:T(128)S(1)}, s32[4]{0:T(128)}, u32[]{:S(2)}) copy-start(s32[4]{0:T(128)} %param.13) | copy-start | bytes 52
  17.6 10.2 %copy-start.4 = (s32[4]{0:T(128)S(1)}, s32[4]{0:T(128)}, u32[]{:S(2)}) copy-start(s32[4]{0:T(128)} %param.14) | copy-start | bytes 52
  17.7 10.7 %copy-start.2 = (s32[4,2,2]{0,2,1:T(2,128)S(1)}, s32[4,2,2]{0,2,1:T(2,128)}, u32[]{:S(2)}) copy-start(s32[4,2,2]{0,2,1:T(2,128)} %param.15) | copy-start | bytes 196
  18.7 32.7 %all-to-all-start = ((bf16[2,2,4,2,128,128]{5,4,3,1,0,2:T(8,128)(2,1)}), bf16[2,2,4,2,128,128]{5,4,3,1,0,2:T(8,128)(2,1)S(1)}, u32[]{:S(2)}, u32[]{:S(2)}) async-start(bf16[2,2,4,2,128,128]{5,4,3,1,0,2:T(8,128)(2,1)} %copy.77), calls=%async_computation | async-start | bytes 2097152 | tf_op jit(solution)/shard_map/all_to_all | solution.py:87
  25.1 33.2 %collective-permute-start = (bf16[1,2,128,4,128]{4,2,3,1,0:T(8,128)(2,1)S(1)}, bf16[1,2,128,4,128]{4,2,3,1,0:T(8,128)(2,1)S(1)}, u32[]{:S(2)}, u32[]{:S(2)}) collective-permute-start(bf16[1,2,128,4,128]{4,2,3,1,0:T(8,128)(2,1)S(1)} %copy.111), channel_id=1, source_target_pairs={{0,1},{2,3},{4,5},{6,7},{8,9},{10,11},{12,13},{14,15},{16,17},{18,... | collective-permute-start | bytes 786440 | tf_op jit(solution)/shard_map/ppermute | solution.py:10
  29.9 27.2 %copy-start.1 = (bf16[1,128,16,128]{3,2,1,0:T(8,128)(2,1)S(1)}, bf16[1,128,16,128]{3,2,1,0:T(8,128)(2,1)}, u32[]{:S(2)}) copy-start(bf16[1,128,16,128]{3,2,1,0:T(8,128)(2,1)} %param.9) | copy-start | bytes 1572868
  51.4 17.7 %all-to-all-start.2 = ((bf16[2,2,4,1,128,128]{5,4,1,0,3,2:T(8,128)(2,1)}), bf16[2,2,4,1,128,128]{5,4,1,0,3,2:T(8,128)(2,1)S(1)}, u32[]{:S(2)}, u32[]{:S(2)}) async-start(bf16[2,2,4,1,128,128]{5,4,1,0,3,2:T(8,128)(2,1)} %copy.89), calls=%async_computation.2 | async-start | bytes 1048576 | tf_op jit(solution)/shard_map/all_to_all | solution.py:88
  54.9 15.5 %all-gather.2.cloned.1.call-start = ((), (), s32[]{:S(2)}) async-start(), calls=%async_computation.3 | async-start | bytes 3145728 | tf_op jit(solution)/shard_map/all_gather | solution.py:101
Sparse Core Ops, SparseCore 0:
  57.3 12.0 all-gather.1
where the time goes:
time: 239 us; the launch traced here: 236 us
  local copies, waits for them, and re-layouts  72.4 us (30%)
  loops' own time  67.1 us (28%)
  waiting for transfers between devices  30.7 us (13%)
  matrix products  24 us (10%)
  starting transfers between devices  15.4 us (6%)
  between operations  14.8 us (6%)
  other arithmetic  11.6 us (5%)
    another operation x1, loops' own time, attend(): return lax.map(one_head, jnp.arange(query_rows.shape[1]))  67.1 us
    dynamic_update_slice x32, local copies, waits for them, and re-layouts, attend(): return lax.map(one_head, jnp.arange(query_rows.shape[1]))  46.5 us
    all_to_all x1, waiting for transfers between devices, body(): lax.all_to_all(outgoing, 'pool', split_axis=2, concat_axis=2, tiled=True)  19.8 us
    dot_general x16, matrix products, one_head(): jnp.einsum('rd,kd->rk', query_head, keys_head, preferred_element_type=jnp...  17.8 us
    all_to_all x1, waiting for transfers between devices, body(): lax.all_to_all(push_out, 'pool', split_axis=2, concat_axis=2, tiled=True)  10.9 us
    dynamic_slice x16, local copies, waits for them, and re-layouts, attend(): return lax.map(one_head, jnp.arange(query_rows.shape[1]))  10.7 us
    all_to_all x1, starting transfers between devices, body(): lax.all_to_all(outgoing, 'pool', split_axis=2, concat_axis=2, tiled=True)  6.32 us
    dot_general x16, matrix products, one_head(): result = jnp.dot(weights, values_head, preferred_element_type=jnp.float32)  5.05 us
  transfers between devices with their start and end apart: 5, of which 2 were waited for; matrix products, arithmetic and copies ran while one was open for 6% of the time, Pallas kernels for 0%

commit v1 on v0

v1 whole, which is shorter than its diff:
```python
import functools
import math

import jax
import jax.numpy as jnp
from jax import lax
from jax.experimental import pallas as pl
from jax.experimental.pallas import tpu as pltpu
from jax.sharding import PartitionSpec as P

MESH = pl.DeviceIdType.MESH
LOG2E = math.log2(math.e)
LN2 = math.log(2.0)


def kernel(
    sizes, tab, q_ref, sk_ref, store_ref, attn_ref, lse_ref, fresh_ref,
    pages, outbox, kv, sfx, freshbox, landed, qf, skf, qb, acc, top, total,
    load_sem, page_send, page_recv, pass_send, pass_recv,
    sfx_send, sfx_recv, fresh_send, fresh_recv,
):
    n, requests, cap, spages, level_count, heads, kv_all, kv_dev, page, hd = sizes
    rows = page
    group = heads // kv_all
    me = lax.axis_index("pool")
    seq = lax.axis_index("seq")
    other = 1 - seq
    base_prefix = requests * cap * 2
    base_suffix = base_prefix + requests
    base_alloc = base_suffix + requests
    far_right = me < n // 2

    def partner(k):
        high = n - 1 - k
        right = jnp.where(high > me, high, high - 1)
        left = jnp.where(k < me, k, k + 1)
        return jnp.where(far_right, right, left)

    load = pltpu.make_async_copy(store_ref, pages, load_sem)
    load.start()

    barrier = pltpu.get_barrier_semaphore()

    def greet(k, c):
        pl.semaphore_signal(barrier, inc=1, device_id={"pool": partner(k)}, device_id_type=MESH)
        return c

    lax.fori_loop(0, n - 1, greet, 0)
    pl.semaphore_signal(barrier, inc=1, device_id={"seq": other}, device_id_type=MESH)
    pl.semaphore_wait(barrier, n)
    load.wait()

    def slots_of(request):
        live = tab[base_prefix + request]

        def step(p, state):
            count, picks = state
            at = (request * cap + p) * 2
            mine = (tab[at] == me) & (p < live)
            slot = tab[at + 1]
            picks = tuple(
                jnp.where(mine & (count == level), slot, picks[level]) for level in range(level_count)
            )
            return count + mine.astype(jnp.int32), picks

        zero = jnp.int32(0)
        return lax.fori_loop(0, cap, step, (zero, (zero,) * level_count), unroll=cap <= 8)[1]

    def page_copy(k):
        to = partner(k)
        return pltpu.make_async_remote_copy(
            src_ref=outbox.at[to], dst_ref=kv.at[me, seq],
            send_sem=page_send.at[to], recv_sem=page_recv.at[me],
            device_id={"pool": to}, device_id_type=MESH,
        )

    def page_arrival(source):
        return pltpu.make_async_remote_copy(
            src_ref=outbox.at[source], dst_ref=kv.at[source, seq],
            send_sem=page_send.at[source], recv_sem=page_recv.at[source],
            device_id={"pool": source}, device_id_type=MESH,
        )

    def pass_copy(source, half):
        return pltpu.make_async_remote_copy(
            src_ref=kv.at[source, half], dst_ref=kv.at[source, half],
            send_sem=pass_send.at[source], recv_sem=pass_recv.at[source],
            device_id={"seq": other}, device_id_type=MESH,
        )

    def send_pages(k, c):
        to = partner(k)
        picks = slots_of(to)
        for level in range(level_count):
            outbox[to, :, :, level * page:(level + 1) * page, :] = pages[picks[level]]
        page_copy(k).start()
        return c

    lax.fori_loop(0, n - 1, send_pages, 0)

    picks = slots_of(me)
    for level in range(level_count):
        kv[me, seq, :, :, level * page:(level + 1) * page, :] = pages[picks[level]]
    pass_copy(me, seq).start()

    skf[...] = sk_ref[...].astype(jnp.float32)
    for a in range(2):
        for h in range(kv_all):
            picked = skf[pl.ds(a * rows * kv_all + h, rows, stride=kv_all), :]
            sfx[seq, a, h] = picked.astype(jnp.bfloat16)

    def sfx_copy(half):
        return pltpu.make_async_remote_copy(
            src_ref=sfx.at[half], dst_ref=sfx.at[half],
            send_sem=sfx_send, recv_sem=sfx_recv,
            device_id={"seq": other}, device_id_type=MESH,
        )

    sfx_copy(seq).start()
    sfx_copy(other).wait_recv()

    def fresh_pick(to):
        pick = jnp.int32(0)
        for q in range(1, spages):
            pick = jnp.where(tab[base_alloc + (me * spages + q) * 2] == to, q, pick)
        return sfx[pick, :, pl.ds(seq * kv_dev, kv_dev)]

    def fresh_copy(to, source, at):
        return pltpu.make_async_remote_copy(
            src_ref=freshbox.at[to], dst_ref=landed.at[source],
            send_sem=fresh_send.at[to], recv_sem=fresh_recv.at[source],
            device_id={"pool": at}, device_id_type=MESH,
        )

    def send_fresh(k, c):
        to = partner(k)
        freshbox[to] = fresh_pick(to)
        fresh_copy(to, me, to).start()
        return c

    lax.fori_loop(0, n - 1, send_fresh, 0)
    landed[me] = fresh_pick(me)

    qf[...] = q_ref[...].astype(jnp.float32)
    for h in range(heads):
        qb[h * rows:(h + 1) * rows, :] = qf[pl.ds(h, rows, stride=heads), :].astype(jnp.bfloat16)

    scale = (hd ** -0.5) * LOG2E

    def attend(j, keys, values, seen, first):
        at = slice(j * group * rows, (j + 1) * group * rows)
        scores = lax.dot_general(
            qb[at, :], keys, (((1,), (1,)), ((), ())), preferred_element_type=jnp.float32
        ) * scale
        scores = jnp.where(seen, scores, -jnp.inf)
        peak = jnp.max(scores, axis=1, keepdims=True)
        if not first:
            before = top[at, :]
            peak = jnp.maximum(before, peak)
        weights = jnp.exp2(scores - peak)
        mass = jnp.sum(weights, axis=1, keepdims=True)
        result = jnp.dot(weights.astype(jnp.bfloat16), values, preferred_element_type=jnp.float32)
        if first:
            total[at, :] = mass
            acc[at, :] = result
        else:
            fade = jnp.exp2(before - peak)
            total[at, :] = total[at, :] * fade + mass
            acc[at, :] = acc[at, :] * fade + result
        top[at, :] = peak

    block = (group * rows, spages * rows)
    token = lax.broadcasted_iota(jnp.int32, block, 0) % rows
    causal = lax.broadcasted_iota(jnp.int32, block, 1) <= token + seq * rows
    for j in range(kv_all):
        keys = sfx[:, 0, j].reshape(spages * rows, hd)
        values = sfx[:, 1, j].reshape(spages * rows, hd)
        attend(j, keys, values, causal, True)

    live_mine = tab[base_prefix + me]

    def attend_source(source):
        def step(p, count):
            hit = (tab[(me * cap + p) * 2] == source) & (p < live_mine)
            return count + hit.astype(jnp.int32)

        count = lax.fori_loop(0, cap, step, jnp.int32(0), unroll=cap <= 8)
        shape = (group * rows, level_count * page)
        seen = lax.broadcasted_iota(jnp.int32, shape, 1) < count * page
        for j in range(kv_all):
            attend(
                j, kv[source, j // kv_dev, 0, j % kv_dev], kv[source, j // kv_dev, 1, j % kv_dev],
                seen, False,
            )

    pass_copy(me, other).wait_recv()
    attend_source(me)

    def visit(k, c):
        source = partner(k)
        page_arrival(source).wait_recv()
        pass_copy(source, seq).start()
        pass_copy(source, other).wait_recv()
        attend_source(source)
        return c

    lax.fori_loop(0, n - 1, visit, 0)

    suffix_mine = tab[base_suffix + me]
    ids = lax.broadcasted_iota(jnp.int32, (rows, hd), 0)
    live = ids + seq * rows < suffix_mine * page
    eye = ids == lax.broadcasted_iota(jnp.int32, (rows, hd), 1)
    lane = lax.broadcasted_iota(jnp.int32, (1, rows), 1)
    for h in range(heads):
        at = slice(h * rows, (h + 1) * rows)
        mass = total[at, :]
        qf[pl.ds(h, rows, stride=heads), :] = jnp.where(live, acc[at, :] / mass, 0.0)
        lse = top[at, :] * LN2 + jnp.log(mass)
        line = jnp.sum(jnp.where(eye, lse, 0.0), axis=0, keepdims=True)
        lse_ref[h:h + 1, :] = jnp.where(lane + seq * rows < suffix_mine * page, line, 0.0)
    attn_ref[...] = qf[...].astype(jnp.bfloat16)

    def fresh_wait(k, c):
        source = partner(k)
        fresh_copy(source, source, source).wait_recv()
        return c

    lax.fori_loop(0, n - 1, fresh_wait, 0)
    for slot in range(spages):
        def find(r, state):
            source, filled = state
            hit = tab[base_alloc + (r * spages + slot) * 2] == me
            alive = hit & (slot < tab[base_suffix + r])
            return jnp.where(hit, r, source), jnp.where(alive, 1, filled)

        source, filled = lax.fori_loop(
            0, requests, find, (jnp.int32(0), jnp.int32(0)), unroll=requests <= 8
        )
        arrived = landed[source]
        fresh_ref[slot] = jnp.where(filled > 0, arrived, jnp.zeros_like(arrived))

    def drain(k, c):
        to = partner(k)
        page_copy(k).wait_send()
        fresh_copy(to, me, to).wait_send()
        pass_copy(to, seq).wait_send()
        return c

    lax.fori_loop(0, n - 1, drain, 0)
    pass_copy(me, seq).wait_send()
    sfx_copy(seq).wait_send()


def body(queries, suffix_kv, page_store, holder_table, prefix_pages, suffix_pages, fresh_alloc):
    n = lax.axis_size("pool")
    halves = lax.axis_size("seq")
    slots, _, kv_dev, page, hd = page_store.shape
    requests, cap = holder_table.shape[:2]
    spages = fresh_alloc.shape[1]
    levels = cap // n
    rows, heads = queries.shape[1:3]
    kv_all = suffix_kv.shape[3]
    assert requests == n and rows == page and spages == halves == 2
    assert kv_all == kv_dev * halves
    tab = jnp.concatenate(
        [holder_table.reshape(-1), prefix_pages, suffix_pages, fresh_alloc.reshape(-1)]
    )
    sizes = (n, requests, cap, spages, levels, heads, kv_all, kv_dev, page, hd)
    bf16, f32 = jnp.bfloat16, jnp.float32
    dma = pltpu.SemaphoreType.DMA
    vmem = pl.BlockSpec(memory_space=pltpu.VMEM)
    flops = 4 * heads * rows * hd * (cap * page + spages * rows)
    attention, row_lse, fresh = pl.pallas_call(
        functools.partial(kernel, sizes),
        out_shape=(
            jax.ShapeDtypeStruct((rows * heads, hd), bf16),
            jax.ShapeDtypeStruct((heads, rows), f32),
            jax.ShapeDtypeStruct((spages, 2, kv_dev, page, hd), bf16),
        ),
        in_specs=[
            pl.BlockSpec(memory_space=pltpu.SMEM), vmem, vmem, pl.BlockSpec(memory_space=pl.ANY),
        ],
        out_specs=(vmem, vmem, vmem),
        scratch_shapes=[
            pltpu.VMEM((slots, 2, kv_dev, page, hd), bf16),
            pltpu.VMEM((n, 2, kv_dev, levels * page, hd), bf16),
            pltpu.VMEM((n, halves, 2, kv_dev, levels * page, hd), bf16),
            pltpu.VMEM((halves, 2, kv_all, rows, hd), bf16),
            pltpu.VMEM((n, 2, kv_dev, page, hd), bf16),
            pltpu.VMEM((n, 2, kv_dev, page, hd), bf16),
            pltpu.VMEM((rows * heads, hd), f32),
            pltpu.VMEM((2 * rows * kv_all, hd), f32),
            pltpu.VMEM((rows * heads, hd), bf16),
            pltpu.VMEM((rows * heads, hd), f32),
            pltpu.VMEM((rows * heads, 1), f32),
            pltpu.VMEM((rows * heads, 1), f32),
            dma, dma((n,)), dma((n,)), dma((n,)), dma((n,)),
            dma, dma, dma((n,)), dma((n,)),
        ],
        compiler_params=pltpu.CompilerParams(
            collective_id=0, has_side_effects=True, vmem_limit_bytes=58 * 1024 * 1024
        ),
        cost_estimate=pl.CostEstimate(
            flops=flops, bytes_accessed=6 * 1024 * 1024, transcendentals=flops // (4 * hd)
        ),
        name="suffix_attention",
    )(tab, queries.reshape(rows * heads, hd), suffix_kv.reshape(2 * rows * kv_all, hd), page_store)
    return (
        attention.reshape(1, rows, heads, hd), row_lse[None], fresh,
    )


def solution(mesh):
    placed = (
        P(("replica", "pool"), "seq", "tensor", None),
        P(("replica", "pool"), None, "seq", "tensor", None),
        P(("replica", "pool"), None, ("tensor", "seq"), None, None),
        P("replica", None, None),
        P("replica"),
        P("replica"),
        P("replica", None, None),
    )
    return jax.shard_map(
        body,
        mesh=mesh,
        in_specs=placed,
        out_specs=(
            P(("replica", "pool"), "seq", "tensor", None),
            P(("replica", "pool"), "tensor", "seq"),
            P(("replica", "pool"), None, ("tensor", "seq"), None, None),
        ),
        check_vma=False,
    )
```

time: 239 us -> 53.8 us (0.23)
  the two profiles are of different devices: /device:TPU:0 before, /device:TPU:8 now
where the time goes in v1:
time: 53.8 us; the launch traced here: 53.4 us
  Pallas kernels  45 us (84%)
  local copies, waits for them, and re-layouts  6.58 us (12%)
  other arithmetic  1.26 us (2%)
  between operations  0.64 us (1%)
    pallas_call x1, Pallas kernels, body(): pl.pallas_call(functools.partial(kernel, sizes), out_shape=(jax.ShapeDtyp...  45 us
    unnamed x5, local copies, waits for them, and re-layouts  6.39 us
    concatenate x1, other arithmetic, body(): jnp.concatenate([holder_table.reshape(-1), prefix_pages, suffix_pages, fr...  1.26 us

profile of v1, /device:TPU:8, one launch (start us, length us, event | category | flops | bytes accessed | tf_op | source)
XLA Modules:
  0.0 53.4 jit_solution(1844975850585573186)
XLA Ops:
  0.6 0.8 %copy.13 = s32[4,2,2]{2,1,0:T(2,128)S(1)} copy(s32[4,2,2]{0,2,1:T(2,128)} %param.13) | data formatting | bytes 128 | tf_op args[6]
  1.4 0.1 reshape.22
  1.5 0.8 %copy.12 = s32[4,8,2]{2,1,0:T(8,128)S(1)} copy(s32[4,8,2]{1,2,0:T(2,128)} %param.10) | data formatting | bytes 512 | tf_op args[3]
  2.3 0.1 reshape.21
  2.4 1.3 %pad_add_fusion.tab = s32[88]{0:T(128)} fusion(s32[16]{0:T(128)S(1)} %reshape.22, s32[4]{0:T(128)} %param.12, s32[4]{0:T(128)} %param.11, s32[64]{0:T(128)S(1)} %reshape.21), kind=kLoop, calls=%fused_computation | loop fusion | flops 264 | bytes 704 | tf_op jit(solution)/shard_map/concatenate | solution.py:265
  3.6 45.0 %suffix_attention.1 = (bf16[2048,128]{1,0:T(8,128)(2,1)}, f32[16,128]{1,0:T(8,128)}, bf16[2,2,2,128,128]{4,3,2,1,0:T(8,128)(2,1)}) custom-call(s32[88]{0:T(128)} %pad_add_fusion.tab, bf16[2048,128]{1,0:T(8,128)(2,1)} %bitcast.4, bf16[1024,128]{1,0:T(8,128)(2,1)} %bitcast.6, bf16[32,2,2,128,128]{4,3,2,1,0:T(8,128)(2,1)} %store_ref.1), custom_call_target="tpu_custom_call" | custom-call | flops 1342177280 | bytes 6291456 | tf_op jit(solution)/shard_map/suffix_attention/pallas_call | solution.py:273
  48.6 1.9 %copy.17 = bf16[1,128,16,128]{3,2,1,0:T(8,128)(2,1)} copy(bf16[1,128,16,128]{3,2,1,0:T(8,128)(2,1)} %bitcast.5) | data formatting | bytes 1048576
  50.5 1.3 %copy.18 = f32[1,16,128]{2,1,0:T(8,128)} copy(f32[1,16,128]{2,1,0:T(8,128)} %bitcast.7) | data formatting | bytes 16384
  51.8 1.7 %copy.19 = bf16[2,2,2,128,128]{4,3,2,1,0:T(8,128)(2,1)} copy(bf16[2,2,2,128,128]{4,3,2,1,0:T(8,128)(2,1)} %get-tuple-element.14) | data formatting | bytes 524288

commit v2 on v1

v2 whole, which is shorter than its diff:
```python
import functools
import math

import jax
import jax.numpy as jnp
from jax import lax
from jax.experimental import pallas as pl
from jax.experimental.pallas import tpu as pltpu
from jax.sharding import PartitionSpec as P

MESH = pl.DeviceIdType.MESH
LOG2E = math.log2(math.e)
LN2 = math.log(2.0)


def kernel(
    sizes, table, prefix, suffix, alloc, q_hbm, sk_hbm, store_ref,
    attn_ref, lse_ref, landed,
    pages, outbox, kv, sfx, freshbox, qin, skin, attn, lse_rows, qf, skf, qb, acc, top, total,
    load_sem, q_sem, sk_sem, attn_sem, lse_sem, own_sem, page_send, page_recv, pass_send, pass_recv,
    sfx_send, sfx_recv, fresh_send, fresh_recv,
):
    n, requests, cap, spages, level_count, heads, kv_all, kv_dev, page, hd = sizes
    rows = page
    group = heads // kv_all
    me = lax.axis_index("pool")
    seq = lax.axis_index("seq")
    other = 1 - seq
    far_right = me < n // 2

    def partner(k):
        high = n - 1 - k
        right = jnp.where(high > me, high, high - 1)
        left = jnp.where(k < me, k, k + 1)
        return jnp.where(far_right, right, left)

    load = pltpu.make_async_copy(store_ref, pages, load_sem)
    load.start()
    q_load = pltpu.make_async_copy(q_hbm, qin, q_sem)
    sk_load = pltpu.make_async_copy(sk_hbm, skin, sk_sem)
    sk_load.start()
    q_load.start()

    barrier = pltpu.get_barrier_semaphore()

    def greet(k, c):
        pl.semaphore_signal(barrier, inc=1, device_id={"pool": partner(k)}, device_id_type=MESH)
        return c

    lax.fori_loop(0, n - 1, greet, 0)
    pl.semaphore_signal(barrier, inc=1, device_id={"seq": other}, device_id_type=MESH)
    pl.semaphore_wait(barrier, n)
    load.wait()

    def slots_of(request):
        live = prefix[request]

        def step(p, state):
            count, picks = state
            mine = (table[request, 0, p] == me) & (p < live)
            slot = table[request, 1, p]
            picks = tuple(
                jnp.where(mine & (count == level), slot, picks[level]) for level in range(level_count)
            )
            return count + mine.astype(jnp.int32), picks

        zero = jnp.int32(0)
        return lax.fori_loop(0, cap, step, (zero, (zero,) * level_count), unroll=cap <= 8)[1]

    def page_copy(k):
        to = partner(k)
        return pltpu.make_async_remote_copy(
            src_ref=outbox.at[to], dst_ref=kv.at[me, seq],
            send_sem=page_send.at[to], recv_sem=page_recv.at[me],
            device_id={"pool": to}, device_id_type=MESH,
        )

    def page_arrival(source):
        return pltpu.make_async_remote_copy(
            src_ref=outbox.at[source], dst_ref=kv.at[source, seq],
            send_sem=page_send.at[source], recv_sem=page_recv.at[source],
            device_id={"pool": source}, device_id_type=MESH,
        )

    def pass_copy(source, half):
        return pltpu.make_async_remote_copy(
            src_ref=kv.at[source, half], dst_ref=kv.at[source, half],
            send_sem=pass_send.at[source], recv_sem=pass_recv.at[source],
            device_id={"seq": other}, device_id_type=MESH,
        )

    def send_pages(k, c):
        to = partner(k)
        picks = slots_of(to)
        for level in range(level_count):
            outbox[to, :, :, level * page:(level + 1) * page, :] = pages[picks[level]]
        page_copy(k).start()
        return c

    lax.fori_loop(0, n - 1, send_pages, 0)

    picks = slots_of(me)
    for level in range(level_count):
        kv[me, seq, :, :, level * page:(level + 1) * page, :] = pages[picks[level]]
    pass_copy(me, seq).start()

    sk_load.wait()
    skf[...] = skin[...].astype(jnp.float32)
    for a in range(2):
        for h in range(kv_all):
            picked = skf[pl.ds(a * rows * kv_all + h, rows, stride=kv_all), :]
            sfx[seq, a, h] = picked.astype(jnp.bfloat16)

    def sfx_copy(half):
        return pltpu.make_async_remote_copy(
            src_ref=sfx.at[half], dst_ref=sfx.at[half],
            send_sem=sfx_send, recv_sem=sfx_recv,
            device_id={"seq": other}, device_id_type=MESH,
        )

    sfx_copy(seq).start()
    sfx_copy(other).wait_recv()

    def fresh_pick(to):
        pick = jnp.int32(0)
        for q in range(1, spages):
            pick = jnp.where(alloc[q, 0, me] == to, q, pick)
        return sfx[pick, :, pl.ds(seq * kv_dev, kv_dev)]

    def fresh_copy(to, source, at):
        return pltpu.make_async_remote_copy(
            src_ref=freshbox.at[to], dst_ref=landed.at[source],
            send_sem=fresh_send.at[to], recv_sem=fresh_recv.at[source],
            device_id={"pool": at}, device_id_type=MESH,
        )

    def send_fresh(k, c):
        to = partner(k)
        freshbox[to] = fresh_pick(to)
        fresh_copy(to, me, to).start()
        return c

    lax.fori_loop(0, n - 1, send_fresh, 0)
    freshbox[me] = fresh_pick(me)
    own_fresh = pltpu.make_async_copy(freshbox.at[me], landed.at[me], own_sem)
    own_fresh.start()

    q_load.wait()
    qf[...] = qin[...].astype(jnp.float32)
    for h in range(heads):
        qb[h * rows:(h + 1) * rows, :] = qf[pl.ds(h, rows, stride=heads), :].astype(jnp.bfloat16)

    scale = (hd ** -0.5) * LOG2E

    def attend(j, score_parts, values, biases, first):
        peaks = [jnp.max(part, axis=0, keepdims=True) for part in score_parts]
        peaks = [peak if bias is None else peak + bias for peak, bias in zip(peaks, biases)]
        peak = functools.reduce(jnp.maximum, peaks)
        if not first:
            before = top[j]
            peak = jnp.maximum(before, peak)
        weights = jnp.concatenate([
            jnp.exp2(part - (peak if bias is None else peak - bias))
            for part, bias in zip(score_parts, biases)
        ], axis=0)
        mass = jnp.sum(weights, axis=0, keepdims=True)
        result = lax.dot_general(
            values, weights.astype(jnp.bfloat16), (((0,), (0,)), ((), ())),
            preferred_element_type=jnp.float32,
        )
        if first:
            total[j] = mass
            acc[j] = result
        else:
            fade = jnp.exp2(before - peak)
            total[j] = total[j] * fade + mass
            acc[j] = acc[j] * fade + result
        top[j] = peak

    def score(j, keys):
        return lax.dot_general(
            keys, qb[j * group * rows:(j + 1) * group * rows, :], (((1,), (1,)), ((), ())),
            preferred_element_type=jnp.float32,
        ) * scale

    block = (spages * rows, group * rows)
    token = lax.broadcasted_iota(jnp.int32, block, 1) % rows
    causal = lax.broadcasted_iota(jnp.int32, block, 0) <= token + seq * rows
    for j in range(kv_all):
        keys = sfx[:, 0, j].reshape(spages * rows, hd)
        values = sfx[:, 1, j].reshape(spages * rows, hd)
        attend(j, [jnp.where(causal, score(j, keys), -jnp.inf)], values, [None], True)

    live_mine = prefix[me]

    def attend_source(source):
        def step(p, count):
            hit = (table[me, 0, p] == source) & (p < live_mine)
            return count + hit.astype(jnp.int32)

        count = lax.fori_loop(0, cap, step, jnp.int32(0), unroll=cap <= 8)
        biases = [
            jnp.where(count > level, jnp.float32(0.0), jnp.float32(-jnp.inf))
            for level in range(level_count)
        ]
        for j in range(kv_all):
            scores = score(j, kv[source, j // kv_dev, 0, j % kv_dev])
            parts = [scores[level * page:(level + 1) * page] for level in range(level_count)]
            attend(j, parts, kv[source, j // kv_dev, 1, j % kv_dev], biases, False)

    pass_copy(me, other).wait_recv()
    attend_source(me)

    def visit(k, c):
        source = partner(k)
        page_arrival(source).wait_recv()
        pass_copy(source, seq).start()
        pass_copy(source, other).wait_recv()
        attend_source(source)
        return c

    lax.fori_loop(0, n - 1, visit, 0)

    suffix_mine = suffix[me]
    ids = lax.broadcasted_iota(jnp.int32, (rows, hd), 0)
    live = ids + seq * rows < suffix_mine * page
    lane = lax.broadcasted_iota(jnp.int32, (1, rows), 1)
    for j in range(kv_all):
        mass = total[j]
        lse = top[j] * LN2 + jnp.log(mass)
        result = acc[j] / mass
        for g in range(group):
            h = j * group + g
            at = slice(g * rows, (g + 1) * rows)
            qf[pl.ds(h, rows, stride=heads), :] = jnp.where(live, result[:, at].T, 0.0)
            lse_rows[h:h + 1, :] = jnp.where(lane + seq * rows < suffix_mine * page, lse[:, at], 0.0)
    attn[...] = qf[...].astype(jnp.bfloat16)
    attn_out = pltpu.make_async_copy(attn, attn_ref, attn_sem)
    lse_out = pltpu.make_async_copy(lse_rows, lse_ref, lse_sem)
    attn_out.start()
    lse_out.start()

    def fresh_wait(k, c):
        source = partner(k)
        fresh_copy(source, source, source).wait_recv()
        return c

    lax.fori_loop(0, n - 1, fresh_wait, 0)
    def drain(k, c):
        to = partner(k)
        page_copy(k).wait_send()
        fresh_copy(to, me, to).wait_send()
        pass_copy(to, seq).wait_send()
        return c

    lax.fori_loop(0, n - 1, drain, 0)
    pass_copy(me, seq).wait_send()
    sfx_copy(seq).wait_send()
    own_fresh.wait()
    attn_out.wait()
    lse_out.wait()


def place(spages, requests, alloc, suffix, attn_in, lse_in, landed, attn_ref, lse_ref, fresh_ref,
          attn, lse, fresh, in_sem, out_sem, fresh_in, fresh_out):
    me = lax.axis_index("pool")
    parts = attn.shape[0]
    attn_loads = [
        pltpu.make_async_copy(attn_in.at[i], attn.at[i], in_sem.at[i]) for i in range(parts)
    ]
    attn_stores = [
        pltpu.make_async_copy(attn.at[i], attn_ref.at[i], out_sem.at[i]) for i in range(parts)
    ]
    lse_load = pltpu.make_async_copy(lse_in, lse, in_sem.at[parts])
    lse_store = pltpu.make_async_copy(lse, lse_ref, out_sem.at[parts])
    for load in attn_loads:
        load.start()
    lse_load.start()
    found = []
    for slot in range(spages):
        def find(r, state):
            source, filled = state
            hit = alloc[slot, 0, r] == me
            alive = hit & (slot < suffix[r])
            return jnp.where(hit, r, source), jnp.where(alive, 1, filled)

        found.append(lax.fori_loop(
            0, requests, find, (jnp.int32(0), jnp.int32(0)), unroll=requests <= 8
        ))
    fresh_loads = [
        pltpu.make_async_copy(landed.at[found[i][0]], fresh.at[i], fresh_in.at[i])
        for i in range(spages)
    ]
    fresh_stores = [
        pltpu.make_async_copy(fresh.at[i], fresh_ref.at[i], fresh_out.at[i])
        for i in range(spages)
    ]
    for load in fresh_loads:
        load.start()
    for load, store in zip(attn_loads, attn_stores):
        load.wait()
        store.start()
    lse_load.wait()
    lse_store.start()
    for slot in range(spages):
        fresh_loads[slot].wait()

        @pl.when(found[slot][1] == 0)
        def _():
            fresh[slot] = jnp.zeros_like(fresh[slot])

        fresh_stores[slot].start()
    for store in attn_stores + [lse_store] + fresh_stores:
        store.wait()


def body(queries, suffix_kv, page_store, holder_table, prefix_pages, suffix_pages, fresh_alloc):
    n = lax.axis_size("pool")
    halves = lax.axis_size("seq")
    slots, _, kv_dev, page, hd = page_store.shape
    requests, cap = holder_table.shape[:2]
    spages = fresh_alloc.shape[1]
    levels = cap // n
    rows, heads = queries.shape[1:3]
    kv_all = suffix_kv.shape[3]
    assert requests == n and rows == page and spages == halves == 2
    assert kv_all == kv_dev * halves
    table = jnp.transpose(holder_table, (0, 2, 1))
    alloc = jnp.transpose(fresh_alloc, (1, 2, 0))
    sizes = (n, requests, cap, spages, levels, heads, kv_all, kv_dev, page, hd)
    bf16, f32 = jnp.bfloat16, jnp.float32
    dma = pltpu.SemaphoreType.DMA
    smem = pl.BlockSpec(memory_space=pltpu.SMEM)
    away = pl.BlockSpec(memory_space=pl.ANY)
    flops = 4 * heads * rows * hd * (cap * page + spages * rows)
    attention, row_lse, landed = pl.pallas_call(
        functools.partial(kernel, sizes),
        out_shape=(
            jax.ShapeDtypeStruct((rows * heads, hd), bf16),
            jax.ShapeDtypeStruct((heads, rows), f32),
            jax.ShapeDtypeStruct((n, 2, kv_dev, page, hd), bf16),
        ),
        in_specs=[smem, smem, smem, smem, away, away, away],
        out_specs=(away, away, away),
        scratch_shapes=[
            pltpu.VMEM((slots, 2, kv_dev, page, hd), bf16),
            pltpu.VMEM((n, 2, kv_dev, levels * page, hd), bf16),
            pltpu.VMEM((n, halves, 2, kv_dev, levels * page, hd), bf16),
            pltpu.VMEM((halves, 2, kv_all, rows, hd), bf16),
            pltpu.VMEM((n, 2, kv_dev, page, hd), bf16),
            pltpu.VMEM((rows * heads, hd), bf16),
            pltpu.VMEM((2 * rows * kv_all, hd), bf16),
            pltpu.VMEM((rows * heads, hd), bf16),
            pltpu.VMEM((heads, rows), f32),
            pltpu.VMEM((rows * heads, hd), f32),
            pltpu.VMEM((2 * rows * kv_all, hd), f32),
            pltpu.VMEM((rows * heads, hd), bf16),
            pltpu.VMEM((kv_all, hd, heads // kv_all * rows), f32),
            pltpu.VMEM((kv_all, 1, heads // kv_all * rows), f32),
            pltpu.VMEM((kv_all, 1, heads // kv_all * rows), f32),
            dma, dma, dma, dma, dma, dma, dma((n,)), dma((n,)), dma((n,)), dma((n,)),
            dma, dma, dma((n,)), dma((n,)),
        ],
        compiler_params=pltpu.CompilerParams(
            collective_id=0, has_side_effects=True, vmem_limit_bytes=58 * 1024 * 1024
        ),
        cost_estimate=pl.CostEstimate(
            flops=flops, bytes_accessed=6 * 1024 * 1024, transcendentals=flops // (4 * hd)
        ),
        name="suffix_attention",
    )(
        table, prefix_pages, suffix_pages, alloc,
        queries.reshape(rows * heads, hd), suffix_kv.reshape(2 * rows * kv_all, hd), page_store,
    )
    parts = 4
    attention, row_lse, fresh = pl.pallas_call(
        functools.partial(place, spages, requests),
        out_shape=(
            jax.ShapeDtypeStruct((parts, rows * heads // parts, hd), bf16),
            jax.ShapeDtypeStruct((heads, rows), f32),
            jax.ShapeDtypeStruct((spages, 2, kv_dev, page, hd), bf16),
        ),
        in_specs=[smem, smem, away, away, away],
        out_specs=(away, away, away),
        scratch_shapes=[
            pltpu.VMEM((parts, rows * heads // parts, hd), bf16),
            pltpu.VMEM((heads, rows), f32),
            pltpu.VMEM((spages, 2, kv_dev, page, hd), bf16),
            dma((parts + 1,)), dma((parts + 1,)), dma((spages,)), dma((spages,)),
        ],
        compiler_params=pltpu.CompilerParams(has_side_effects=True),
        name="place_outputs",
    )(
        alloc, suffix_pages, attention.reshape(parts, rows * heads // parts, hd), row_lse, landed
    )
    return (
        attention.reshape(1, rows, heads, hd), row_lse[None], fresh,
    )


def solution(mesh):
    placed = (
        P(("replica", "pool"), "seq", "tensor", None),
        P(("replica", "pool"), None, "seq", "tensor", None),
        P(("replica", "pool"), None, ("tensor", "seq"), None, None),
        P("replica", None, None),
        P("replica"),
        P("replica"),
        P("replica", None, None),
    )
    return jax.shard_map(
        body,
        mesh=mesh,
        in_specs=placed,
        out_specs=(
            P(("replica", "pool"), "seq", "tensor", None),
            P(("replica", "pool"), "tensor", "seq"),
            P(("replica", "pool"), None, ("tensor", "seq"), None, None),
        ),
        check_vma=False,
    )
```

time: 53.8 us -> 45 us (0.84)
  local copies, waits for them, and re-layouts: 6.58 us -> 0 us
  other arithmetic: 1.26 us -> 0 us
  Pallas kernels: 45 us -> 44.2 us
    unnamed x5 -> x0, local copies, waits for them, and re-layouts: 6.39 us -> none
    pallas_call x1, Pallas kernels: 45 us -> 41.4 us  [body(): pl.pallas_call(functools.partial(kernel, sizes), out_shape=(jax.ShapeDtyp...]
    pallas_call x0 -> x1, Pallas kernels: none -> 2.72 us  [body(): pl.pallas_call(functools.partial(place, spages, requests), out_shape=(jax...]
    concatenate x1 -> x0, other arithmetic: 1.26 us -> none  [body(): jnp.concatenate([holder_table.reshape(-1), prefix_pages, suffix_pages, fr...]
where the time goes in v2:
time: 45 us; the launch traced here: 44.8 us
  Pallas kernels  44.2 us (98%)
  between operations  0.64 us (1%)
    pallas_call x1, Pallas kernels, body(): pl.pallas_call(functools.partial(kernel, sizes), out_shape=(jax.ShapeDtyp...  41.4 us
    pallas_call x1, Pallas kernels, body(): pl.pallas_call(functools.partial(place, spages, requests), out_shape=(jax...  2.72 us

profile of v2, /device:TPU:8, one launch (start us, length us, event | category | flops | bytes accessed | tf_op | source)
XLA Modules:
  0.0 44.8 jit_solution(5001668503911732258)
XLA Ops:
  0.6 41.4 %suffix_attention.1 = (bf16[2048,128]{1,0:T(8,128)(2,1)}, f32[16,128]{1,0:T(8,128)}, bf16[4,2,2,128,128]{4,3,2,1,0:T(8,128)(2,1)}) custom-call(s32[4,2,8]{2,1,0:T(2,128)} %bitcast.12, s32[4]{0:T(128)} %prefix.1, s32[4]{0:T(128)} %suffix.3, s32[2,2,4]{2,1,0:T(2,128)} %bitcast.10, bf16[2048,128]{1,0:T(8,128)(2,1)} %bitcast.7, bf16[1024,128]{1,0:T(8,128)(2,1)} %bitcast.9, ...), custom_call_target="tpu_custom_call" | custom-call | flops 1342177280 | bytes 6291456 | tf_op jit(solution)/shard_map/suffix_attention/pallas_call | solution.py:336
  42.1 2.7 %place_outputs.1 = (bf16[4,512,128]{2,1,0:T(8,128)(2,1)}, f32[16,128]{1,0:T(8,128)}, bf16[2,2,2,128,128]{4,3,2,1,0:T(8,128)(2,1)}) custom-call(s32[2,2,4]{2,1,0:T(2,128)} %bitcast.11, s32[4]{0:T(128)} %suffix.3, bf16[4,512,128]{2,1,0:T(8,128)(2,1)} %bitcast.8, f32[16,128]{1,0:T(8,128)} %get-tuple-element.10.lse_in, ...), custom_call_target="tpu_custom_call" | custom-call | tf_op jit(solution)/shard_map/place_outputs/pallas_call | solution.py:376

commit v3 on v2

--- a/solution.py
+++ b/solution.py
@@ -208,18 +208,25 @@
             parts = [scores[level * page:(level + 1) * page] for level in range(level_count)]
             attend(j, parts, kv[source, j // kv_dev, 1, j % kv_dev], biases, False)
 
-    pass_copy(me, other).wait_recv()
-    attend_source(me)
-
-    def visit(k, c):
+    def relay(k):
         source = partner(k)
         page_arrival(source).wait_recv()
         pass_copy(source, seq).start()
+
+    pass_copy(me, other).wait_recv()
+    attend_source(me)
+    relay(0)
+
+    def visit(k, c):
+        source = partner(k)
         pass_copy(source, other).wait_recv()
+        relay(k + 1)
         attend_source(source)
         return c
 
-    lax.fori_loop(0, n - 1, visit, 0)
+    lax.fori_loop(0, n - 2, visit, 0)
+    pass_copy(partner(n - 2), other).wait_recv()
+    attend_source(partner(n - 2))
 
     suffix_mine = suffix[me]
     ids = lax.broadcasted_iota(jnp.int32, (rows, hd), 0)

time: 45 us -> 43.9 us (0.976)
  Pallas kernels: 44.2 us -> 42.9 us
    pallas_call x1, Pallas kernels: 41.4 us -> 40.2 us  [body(): pl.pallas_call(functools.partial(kernel, sizes), out_shape=(jax.ShapeDtyp...]
where the time goes in v3:
time: 43.9 us; the launch traced here: 43.5 us
  Pallas kernels  42.9 us (98%)
  between operations  0.64 us (1%)
    pallas_call x1, Pallas kernels, body(): pl.pallas_call(functools.partial(kernel, sizes), out_shape=(jax.ShapeDtyp...  40.2 us
    pallas_call x1, Pallas kernels, body(): pl.pallas_call(functools.partial(place, spages, requests), out_shape=(jax...  2.72 us

profile of v3, /device:TPU:8, one launch (start us, length us, event | category | flops | bytes accessed | tf_op | source)
XLA Modules:
  0.0 43.5 jit_solution(16016669526857334415)
XLA Ops:
  0.6 40.2 %suffix_attention.1 = (bf16[2048,128]{1,0:T(8,128)(2,1)}, f32[16,128]{1,0:T(8,128)}, bf16[4,2,2,128,128]{4,3,2,1,0:T(8,128)(2,1)}) custom-call(s32[4,2,8]{2,1,0:T(2,128)} %bitcast.12, s32[4]{0:T(128)} %prefix.1, s32[4]{0:T(128)} %suffix.3, s32[2,2,4]{2,1,0:T(2,128)} %bitcast.10, bf16[2048,128]{1,0:T(8,128)(2,1)} %bitcast.7, bf16[1024,128]{1,0:T(8,128)(2,1)} %bitcast.9, ...), custom_call_target="tpu_custom_call" | custom-call | flops 1342177280 | bytes 6291456 | tf_op jit(solution)/shard_map/suffix_attention/pallas_call | solution.py:343
  40.8 2.7 %place_outputs.1 = (bf16[4,512,128]{2,1,0:T(8,128)(2,1)}, f32[16,128]{1,0:T(8,128)}, bf16[2,2,2,128,128]{4,3,2,1,0:T(8,128)(2,1)}) custom-call(s32[2,2,4]{2,1,0:T(2,128)} %bitcast.11, s32[4]{0:T(128)} %suffix.3, bf16[4,512,128]{2,1,0:T(8,128)(2,1)} %bitcast.8, f32[16,128]{1,0:T(8,128)} %get-tuple-element.10.lse_in, ...), custom_call_target="tpu_custom_call" | custom-call | tf_op jit(solution)/shard_map/place_outputs/pallas_call | solution.py:383

commit v4 on v3

--- a/solution.py
+++ b/solution.py
@@ -97,12 +97,7 @@
         page_copy(k).start()
         return c
 
-    lax.fori_loop(0, n - 1, send_pages, 0)
-
-    picks = slots_of(me)
-    for level in range(level_count):
-        kv[me, seq, :, :, level * page:(level + 1) * page, :] = pages[picks[level]]
-    pass_copy(me, seq).start()
+    lax.fori_loop(0, n // 2, send_pages, 0)
 
     sk_load.wait()
     skf[...] = skin[...].astype(jnp.float32)
@@ -140,7 +135,14 @@
         fresh_copy(to, me, to).start()
         return c
 
-    lax.fori_loop(0, n - 1, send_fresh, 0)
+    lax.fori_loop(0, n // 2, send_fresh, 0)
+    lax.fori_loop(n // 2, n - 1, send_pages, 0)
+    lax.fori_loop(n // 2, n - 1, send_fresh, 0)
+    picks = slots_of(me)
+    for level in range(level_count):
+        kv[me, seq, :, :, level * page:(level + 1) * page, :] = pages[picks[level]]
+    pass_copy(me, seq).start()
+
     freshbox[me] = fresh_pick(me)
     own_fresh = pltpu.make_async_copy(freshbox.at[me], landed.at[me], own_sem)
     own_fresh.start()

time: 43.9 us -> 43.9 us (level)
  no operation moved by 1% of the time
where the time goes in v4:
time: 43.9 us; the launch traced here: 43.5 us
  Pallas kernels  42.9 us (98%)
  between operations  0.64 us (1%)
    pallas_call x1, Pallas kernels, body(): pl.pallas_call(functools.partial(kernel, sizes), out_shape=(jax.ShapeDtyp...  40.2 us
    pallas_call x1, Pallas kernels, body(): pl.pallas_call(functools.partial(place, spages, requests), out_shape=(jax...  2.7 us

profile of v4, /device:TPU:8, one launch (start us, length us, event | category | flops | bytes accessed | tf_op | source)
XLA Modules:
  0.0 43.5 jit_solution(1245570398929927383)
XLA Ops:
  0.6 40.2 %suffix_attention.1 = (bf16[2048,128]{1,0:T(8,128)(2,1)}, f32[16,128]{1,0:T(8,128)}, bf16[4,2,2,128,128]{4,3,2,1,0:T(8,128)(2,1)}) custom-call(s32[4,2,8]{2,1,0:T(2,128)} %bitcast.12, s32[4]{0:T(128)} %prefix.1, s32[4]{0:T(128)} %suffix.3, s32[2,2,4]{2,1,0:T(2,128)} %bitcast.10, bf16[2048,128]{1,0:T(8,128)(2,1)} %bitcast.7, bf16[1024,128]{1,0:T(8,128)(2,1)} %bitcast.9, ...), custom_call_target="tpu_custom_call" | custom-call | flops 1342177280 | bytes 6291456 | tf_op jit(solution)/shard_map/suffix_attention/pallas_call | solution.py:345
  40.8 2.7 %place_outputs.1 = (bf16[4,512,128]{2,1,0:T(8,128)(2,1)}, f32[16,128]{1,0:T(8,128)}, bf16[2,2,2,128,128]{4,3,2,1,0:T(8,128)(2,1)}) custom-call(s32[2,2,4]{2,1,0:T(2,128)} %bitcast.11, s32[4]{0:T(128)} %suffix.3, bf16[4,512,128]{2,1,0:T(8,128)(2,1)} %bitcast.8, f32[16,128]{1,0:T(8,128)} %get-tuple-element.10.lse_in, ...), custom_call_target="tpu_custom_call" | custom-call | tf_op jit(solution)/shard_map/place_outputs/pallas_call | solution.py:385
